TPU v7x, 512 devices: a whole 4x8x8 slice. The times are simulated.
512 devices in a mesh: dp: 8 (over y), owner: 32 (over x, z), rep: 2 (over core).
Axes of the slice: x: 4, y: 8, z: 8, core: 2. Of those that a mesh axis runs over, the one named last changes fastest.
Arguments:
- gradients: bfloat16 [8, 384, 512, 512], P('dp', None, 'owner', 'rep'), may hold values from -110 to 110
Outputs:
- updates: bfloat16 [384, 512, 512], P('owner', 'dp', 'rep')
All inputs are finite; a program needn't handle non-finite values.
Results may differ from a plain program's by a relative error of at most 0.018.
Values may be sent and summed in bfloat16 or wider, within the bound.
A program may use at most 64 MiB of HBM per device.

v0:
```python
import jax
import jax.numpy as jnp
from jax import lax
from jax.sharding import PartitionSpec as P

BS = 512


def from_partner(value, axis, stride):
    mask = 2**stride
    pairs = [(source, source ^ mask) for source in range(lax.axis_size(axis))]
    return lax.ppermute(value, axis, pairs)


def shifted(matrix, identity):
    return ((5.0 * identity - matrix.astype(jnp.float32)) * 0.25).astype(jnp.bfloat16)


def mat_prod(left, right):
    return jnp.dot(left, right, preferred_element_type=jnp.float32)


def full_root(side_matrix):
    factor = jnp.einsum("ik,jk->ij", side_matrix, side_matrix, preferred_element_type=jnp.float32)
    fourth = 0.4 * jnp.sqrt(jnp.sum(factor * factor) + 1e-06)
    scaled = (factor / fourth).astype(jnp.bfloat16)
    identity = jnp.eye(BS, dtype=jnp.float32)
    first_shift = shifted(scaled, identity)
    square = mat_prod(first_shift, first_shift).astype(jnp.bfloat16)
    fourth_power = mat_prod(square, square).astype(jnp.bfloat16)
    next_scaled = mat_prod(fourth_power, scaled).astype(jnp.bfloat16)
    second_shift = shifted(next_scaled, identity)
    return mat_prod(first_shift, second_shift).astype(jnp.bfloat16)


def full_updates(blocks, replica):
    half = BS // 2
    own_sides = jnp.where(replica == 0, blocks, jnp.swapaxes(blocks, 1, 2))
    roots = jax.vmap(full_root)(own_sides)
    partner = from_partner(roots, "rep", 0)
    left_roots = jnp.where(replica == 0, roots, partner)
    right_roots = jnp.where(replica == 0, partner, roots)
    right_cols = lax.dynamic_slice_in_dim(right_roots, replica * half, half, 2)
    mixed = jnp.einsum(
        "kij,kjl->kil", left_roots, blocks, preferred_element_type=jnp.float32
    ).astype(jnp.bfloat16)
    pieces = jnp.einsum("kij,kjl->kil", mixed, right_cols, preferred_element_type=jnp.float32)
    return (pieces, jnp.sum(pieces * pieces, axis=(1, 2)))


def on_device(gradients):
    local = gradients[0]
    n_data = lax.axis_size("dp")
    n_owners = lax.axis_size("owner")
    replica = lax.axis_index("rep")
    row_part = local.shape[1]
    half = local.shape[2]
    slots = local.shape[0] // n_owners
    grouped = local.reshape(n_owners, slots, row_part, half)
    main_part = grouped[:, :n_data]
    tail_part = grouped[:, n_data:]
    paired = jnp.stack([tail_part, jnp.zeros_like(tail_part)], axis=2)
    paired = paired.reshape(n_owners, n_data, row_part, half)
    arranged = jnp.stack([main_part, paired], axis=2)
    moved = lax.all_to_all(
        lax.all_to_all(arranged, "dp", split_axis=1, concat_axis=1, tiled=True),
        "owner",
        split_axis=0,
        concat_axis=3,
        tiled=True,
    )
    halves = jnp.sum(moved.astype(jnp.float32), axis=(0, 1)).astype(jnp.bfloat16)
    whole = lax.all_gather(halves, "rep", axis=2, tiled=True)
    grad_squares = jnp.sum(jnp.square(whole.astype(jnp.float32)), axis=(1, 2))
    pieces, sums = full_updates(whole, replica)
    totals = lax.psum(sums, "rep")
    scales = jnp.sqrt(grad_squares) / jnp.sqrt(totals + 1e-06)
    main_final = (pieces[0] * scales[0]).astype(jnp.bfloat16)
    tail_final = (pieces[1] * scales[1]).astype(jnp.bfloat16)
    row_share = BS // n_data
    tail_width = tail_final.shape[1]
    back_main, back_tail = (
        lax.all_to_all(
            main_final.reshape(n_data, row_share, half),
            "dp",
            split_axis=0,
            concat_axis=0,
            tiled=True,
        ),
        lax.all_to_all(
            tail_final.reshape(n_data, row_share, tail_width),
            "dp",
            split_axis=0,
            concat_axis=0,
            tiled=True,
        ),
    )
    tail_rows = back_tail.reshape(n_data // 2, 2, row_share, half)[:, 0]
    return jnp.concatenate([back_main, tail_rows], axis=0)


def solution(mesh):
    in_specs = (P("dp", None, "owner", "rep"),)
    out_specs = P("owner", "dp", "rep")
    return jax.shard_map(
        on_device, mesh=mesh, in_specs=in_specs, out_specs=out_specs, check_vma=False
    )
```

profile of v0, /device:TPU:1, one launch (start us, length us, event | category | flops | bytes accessed | tf_op | source)
XLA Modules:
  0.0 296.8 jit_solution(13784190864723955574)
XLA Ops:
  6.5 1.3 slice_bitcast_fusion.1
  7.9 1.8 slice_bitcast_fusion
  10.4 0.4 copy.13
  10.8 100.8 %all_to_all.24 = bf16[32,8,2,16,256]{4,3,0,2,1:T(8,128)(2,1)S(1)} all-to-all(bf16[32,8,2,16,256]{4,3,0,2,1:T(8,128)(2,1)S(1)} %copy.13), channel_id=1, replica_groups=mesh['dp'=8,'owner'=32,'rep'=2] {'dp'}, dimensions={1} | all-to-all | bytes 8388608 | tf_op jit(solution)/shard_map/all_to_all | solution.py:66
  111.7 0.6 copy.14
  112.3 105.1 %all_to_all.25 = bf16[32,8,2,16,256]{4,3,1,2,0:T(8,128)(2,1)} all-to-all(bf16[32,8,2,16,256]{4,3,1,2,0:T(8,128)(2,1)S(1)} %copy.14), channel_id=1, replica_groups=mesh['dp'=8,'owner'=32,'rep'=2] {'owner'}, dimensions={0} | all-to-all | bytes 8388608 | tf_op jit(solution)/shard_map/all_to_all | solution.py:65
  217.4 3.2 %reduce_sum.43 = bf16[32,2,16,256]{3,2,1,0:T(8,128)(2,1)S(1)} reduce(bf16[32,8,2,16,256]{4,3,1,2,0:T(8,128)(2,1)} %all_to_all.25, bf16[]{:T(256)} %constant.6.clone.1), dimensions={1}, to_apply=%region_0.0 | reduce | flops 1835008 | bytes 4718594 | tf_op jit(solution)/shard_map/reduce_sum | solution.py:72
  220.6 1.0 copy.16
  221.8 16.3 %all-gather.2.cloned.1.call-done = bf16[2,512,512]{1,2,0:T(8,128)(2,1)} async-done(((bf16[2,512,256]{1,2,0:T(8,128)(2,1)}), bf16[2,512,512]{1,2,0:T(8,128)(2,1)}) %all-gather.2.cloned.1.call-update) | async-done | bytes 1048592 | tf_op jit(solution)/shard_map/all_gather | solution.py:73
  238.1 1.6 copy.17
  239.7 1.0 multiply_reduce_fusion.1
  241.0 2.8 convolution_convert_fusion.3
  243.9 3.5 %convolution_convert_fusion.1 = bf16[2,512,512]{2,1,0:T(8,128)(2,1)} fusion(bf16[2,512,512]{2,1,0:T(8,128)(2,1)} %convolution_convert_fusion.3, bf16[2,512,512]{2,1,0:T(8,128)(2,1)S(1)} %divide_convert_fusion, f32[512,512]{1,0:T(8,128)S(1)} %fusion.8), kind=kOutput, calls=%fused_computation.8 | convolution fusion | flops 1078984704 | bytes 4194304 | tf_op jit(solution)/shard_map/vmap()/dot_general | solution.py:20
  247.4 2.1 collective-permute-start
  249.5 0.4 multiply_reduce_fusion
  249.9 2.2 collective-permute-done
  252.2 2.2 multiply_reduce_fusion.2
  254.3 2.6 psum.7
  257.0 0.6 fusion.20
  257.6 2.0 fusion.13
  259.6 16.5 %all_to_all.26 = bf16[8,64,256]{2,1,0:T(8,128)(2,1)S(1)} all-to-all(bf16[8,64,256]{2,1,0:T(8,128)(2,1)S(1)} %bitcast.30), channel_id=1, replica_groups=mesh['dp'=8,'owner'=32,'rep'=2] {'dp'}, dimensions={0} | all-to-all | bytes 524288 | tf_op jit(solution)/shard_map/all_to_all | solution.py:90
  276.0 3.4 %all-to-all-start.2 = ((bf16[8,64,256]{2,1,0:T(8,128)(2,1)}), bf16[8,64,256]{2,1,0:T(8,128)(2,1)S(1)}, u32[]{:S(2)}, u32[]{:S(2)}) async-start(bf16[8,64,256]{2,1,0:T(8,128)(2,1)} %bitcast.8), calls=%async_computation.2 | async-start | bytes 524288 | tf_op jit(solution)/shard_map/all_to_all | solution.py:83
  279.5 9.7 %all-to-all-done.2 = bf16[8,64,256]{2,1,0:T(8,128)(2,1)S(1)} async-done(((bf16[8,64,256]{2,1,0:T(8,128)(2,1)}), bf16[8,64,256]{2,1,0:T(8,128)(2,1)S(1)}, u32[]{:S(2)}, u32[]{:S(2)}) %all-to-all-start.2) | async-done | bytes 262176 | tf_op jit(solution)/shard_map/all_to_all | solution.py:83
  289.2 0.8 pad_maximum_fusion.1
  (12 shorter events, 1.2 us)
Async XLA Ops:
  6.5 231.6 %all-gather.2.cloned.1.call-start = ((), (), s32[]{:S(2)}) async-start(), calls=%async_computation.4 | async-start | bytes 1572864 | tf_op jit(solution)/shard_map/all_gather | solution.py:73
  238.1 1.6 copy-start
  247.4 4.8 %collective-permute-start = (bf16[2,512,512]{2,1,0:T(8,128)(2,1)}, bf16[2,512,512]{2,1,0:T(8,128)(2,1)S(1)}, u32[]{:S(2)}, u32[]{:S(2)}) collective-permute-start(bf16[2,512,512]{2,1,0:T(8,128)(2,1)} %convolution_convert_fusion.1), channel_id=1, source_target_pairs={{0,1},{1,0},{2,3},{3,2},{4,5},{5,4},{6,7},{7,6},{8,9},{9,8},{10,11... | collective-permute-start | bytes 3145736 | tf_op jit(solution)/shard_map/ppermute | solution.py:12
  276.0 13.1 %all-to-all-start.2 = ((bf16[8,64,256]{2,1,0:T(8,128)(2,1)}), bf16[8,64,256]{2,1,0:T(8,128)(2,1)S(1)}, u32[]{:S(2)}, u32[]{:S(2)}) async-start(bf16[8,64,256]{2,1,0:T(8,128)(2,1)} %bitcast.8), calls=%async_computation.2 | async-start | bytes 524288 | tf_op jit(solution)/shard_map/all_to_all | solution.py:83
Sparse Core Ops, SparseCore 0:
  221.8 16.2 all-gather.1
where the time goes:
time: 299 us; the launch traced here: 297 us
  blocking collectives  225 us (75%)
  waiting for transfers between devices  28.2 us (9%)
  between operations  13.5 us (5%)
  matrix products  9.51 us (3%)
  local copies, waits for them, and re-layouts  7.72 us (3%)
  other arithmetic  7.24 us (2%)
  starting transfers between devices  5.52 us (2%)
    all_to_all x1, blocking collectives, on_device(): lax.all_to_all(lax.all_to_all(arranged, 'dp', split_axis=1, concat_axis=1...  105 us
    all_to_all x1, blocking collectives, on_device(): lax.all_to_all(arranged, 'dp', split_axis=1, concat_axis=1, tiled=True)  101 us
    all_to_all x1, blocking collectives, on_device(): lax.all_to_all(tail_final.reshape(n_data, row_share, tail_width), 'dp', s...  16.5 us
    all_gather x1, waiting for transfers between devices, on_device(): whole = lax.all_gather(halves, 'rep', axis=2, tiled=True)  16.3 us
    all_to_all x1, waiting for transfers between devices, on_device(): lax.all_to_all(main_final.reshape(n_data, row_share, half), 'dp', split_a...  9.67 us
    dot_general x2, matrix products, mat_prod(): return jnp.dot(left, right, preferred_element_type=jnp.float32)  6.37 us
  transfers between devices with their start and end apart: 3, of which 3 were waited for; matrix products, arithmetic and copies ran while one was open for 0% of the time, Pallas kernels for 0%

commit v1 on v0

v1 whole, which is shorter than its diff:
```python
import functools

import jax
import jax.numpy as jnp
from jax import lax
from jax.experimental import pallas as pl
from jax.experimental.pallas import tpu as pltpu
from jax.sharding import PartitionSpec as P

MESH = pl.DeviceIdType.MESH
BS = 512
HALF = BS // 2
F32 = jnp.float32
BF16 = jnp.bfloat16


def dot(a, b):
    return jnp.dot(a, b, preferred_element_type=F32)


def eye_shift(matrix):
    rows = lax.broadcasted_iota(jnp.int32, matrix.shape, 0)
    cols = lax.broadcasted_iota(jnp.int32, matrix.shape, 1)
    value = matrix.astype(F32) * -0.25
    return jnp.where(rows == cols, value + 1.25, value).astype(BF16)


def kernel(
    n_data,
    n_owners,
    g_ref,
    out_ref,
    own,
    ring_main,
    ring_tail,
    sums_main,
    sums_tail,
    gathered,
    side,
    scaled_ref,
    first_ref,
    root_ref,
    left_in,
    right_in,
    right_half,
    update_ref,
    norm_out,
    norm_in,
    stage,
    load_sem,
    ring_send,
    ring_recv,
    owner_send,
    owner_recv,
    half_send,
    half_recv,
    root_send,
    root_recv,
    norm_send,
    norm_recv,
    back_send,
    back_recv,
):
    y = lax.axis_index("dp")
    me = lax.axis_index("owner")
    r = lax.axis_index("rep")
    parity = lax.rem(me, 2)
    y_parity = lax.rem(y, 2)
    other = 1 - r
    subs = 4
    lead = n_owners // 2
    part = lead // subs
    row_part = BS // n_owners
    share = BS // n_data

    load = pltpu.make_async_copy(g_ref, own, load_sem)
    load.start()

    barrier = pltpu.get_barrier_semaphore()

    @pl.loop(0, n_owners)
    def _(k):
        @pl.when(k != me)
        def _():
            pl.semaphore_signal(barrier, inc=1, device_id=(y, k, r), device_id_type=MESH)

    for step in range(1, n_data):
        pl.semaphore_signal(
            barrier, inc=1, device_id=(lax.rem(y + step, n_data), me, r), device_id_type=MESH
        )
    pl.semaphore_signal(barrier, inc=1, device_id=(y, me, other), device_id_type=MESH)
    pl.semaphore_wait(barrier, n_owners + n_data - 1)

    rings = (ring_main, ring_tail)
    sums = (sums_main, sums_tail)
    neighbours = (lax.rem(y + 1, n_data), lax.rem(y + n_data - 1, n_data))

    def block_part(ref, phase, dest, c):
        lead_part = pl.ds(c * part, part)
        if phase == 0:
            return ref.at[lead_part, :, dest]
        return ref.at[lead_part, lax.rem(dest, 2), n_data + lax.div(dest, 2)]

    def dest_of(way, step):
        ahead = 4 - step if way == 0 else 4 + step
        return lax.rem(y + ahead, n_data)

    def ring_copy(phase, way, step, c, raw):
        ring = rings[phase]
        slot = ring.at[way * 4 + step, pl.ds(c * part, part)]
        if raw:
            source = block_part(g_ref, phase, dest_of(way, step), c)
        else:
            source = ring.at[way * 4 + step - 1, pl.ds(c * part, part)]
        return pltpu.make_async_remote_copy(
            src_ref=source,
            dst_ref=slot,
            send_sem=ring_send.at[phase],
            recv_sem=ring_recv.at[phase, way * 4 + step, c],
            device_id=(neighbours[way], me, r),
            device_id_type=MESH,
        )

    def ring_wait(phase, way, step, c):
        slot = rings[phase].at[way * 4 + step, pl.ds(c * part, part)]
        pltpu.make_async_copy(slot, slot, ring_recv.at[phase, way * 4 + step, c]).wait()

    first = ((0, 1), (2, 3))

    def ring_start(phase):
        for j in range(2):
            for way in range(2):
                ring_copy(phase, way, 0, first[way][j], True).start()
        for j in range(2):
            for way in range(2):
                ring_copy(phase, way, 1, first[1 - way][j], True).start()

    def ring_step(phase, way, step, c):
        ring_wait(phase, way, step, c)
        slot = rings[phase].at[way * 4 + step, pl.ds(c * part, part)]
        slot[...] = slot[...] + block_part(own, phase, dest_of(way, step + 1), c)[...]
        ring_copy(phase, way, step + 1, c, False).start()

    def ring_steps(phase):
        for step in range(3):
            order = (0, 1) if step == 0 else (2, 3, 0, 1)
            for j in order:
                for way in range(2):
                    ring_step(phase, way, step, (first[way] + first[1 - way])[j])

    def to_owner(phase, i, k):
        source = sums[phase].at[i]
        target = gathered.at[phase, r, pl.ds(me * row_part, row_part)]

        @pl.when(k != me)
        def _():
            pltpu.make_async_remote_copy(
                src_ref=source,
                dst_ref=target,
                send_sem=owner_send.at[phase],
                recv_sem=owner_recv.at[phase],
                device_id=(y, k, r),
                device_id_type=MESH,
            ).start()

        @pl.when(k == me)
        def _():
            pltpu.make_async_copy(source, target, owner_recv.at[phase]).start()

    def finish(phase):
        for c in (0, 2, 1, 3):
            for way in range(2):
                ring_wait(phase, way, 3, c)
            lead_part = pl.ds(c * part, part)
            ring = rings[phase]
            total = (
                ring[3, lead_part].astype(F32)
                + ring[7, lead_part].astype(F32)
                + block_part(own, phase, y, c)[...].astype(F32)
            ).astype(BF16)
            count = part * (2 if phase == 0 else 1)
            sums[phase][pl.ds(c * count, count)] = total.reshape(count, row_part, HALF)

            @pl.loop(0, count)
            def _(i):
                at = c * count + i
                k = at if phase == 0 else 2 * at + y_parity
                to_owner(phase, at, k)

    def precondition(phase):
        mine = gathered.at[phase, r]
        pltpu.make_async_copy(mine, mine, owner_recv.at[phase]).wait()
        swap = pltpu.make_async_remote_copy(
            src_ref=mine,
            dst_ref=mine,
            send_sem=half_send.at[phase],
            recv_sem=half_recv.at[phase],
            device_id=(y, me, other),
            device_id_type=MESH,
        )
        swap.start()
        swap.wait()

        @pl.when(r == 0)
        def _():
            for h in range(2):
                side[:, h * HALF : (h + 1) * HALF] = gathered[phase, h]

        @pl.when(r == 1)
        def _():
            for h in range(2):
                side[h * HALF : (h + 1) * HALF, :] = gathered[phase, h].T

        s = side[...]
        grad_squares = jnp.sum(jnp.square(s.astype(F32)), keepdims=True)
        factor = lax.dot_general(s, s, (((1,), (1,)), ((), ())), preferred_element_type=F32)
        fourth = 0.4 * jnp.sqrt(jnp.sum(factor * factor, keepdims=True) + 1e-06)
        scaled = (factor * (1.0 / fourth)).astype(BF16)
        scaled_ref[...] = scaled
        first_ref[...] = eye_shift(scaled)
        square = dot(first_ref[...], first_ref[...]).astype(BF16)
        power = dot(square, square).astype(BF16)
        second = eye_shift(dot(power, scaled_ref[...]).astype(BF16))

        def send_root(source, target, i):
            return pltpu.make_async_remote_copy(
                src_ref=source,
                dst_ref=target,
                send_sem=root_send.at[phase, i],
                recv_sem=root_recv.at[phase, i],
                device_id=(y, me, other),
                device_id_type=MESH,
            )

        def left_copy(h):
            rows = pl.ds(h * HALF, HALF)
            return send_root(root_ref.at[phase, rows], left_in.at[phase, rows], h)

        right_copy = send_root(right_half.at[phase], right_in.at[phase], 0)

        @pl.when(r == 0)
        def _():
            for h in range(2):
                rows = pl.ds(h * HALF, HALF)
                root_ref[phase, rows] = dot(first_ref[rows], second).astype(BF16)
                left_copy(h).start()
            mixed = dot(root_ref[phase], side[...]).astype(BF16)
            right_copy.wait_recv()
            update_ref[...] = dot(mixed, right_in[phase])
            for h in range(2):
                left_copy(h).wait_send()

        @pl.when(r == 1)
        def _():
            right_half[phase] = dot(first_ref[...], second[:, :HALF]).astype(BF16)
            right_copy.start()
            right = dot(first_ref[...], second[:, HALF:]).astype(BF16)
            mixed = (
                dot(gathered[phase, 0], right[:HALF]) + dot(gathered[phase, 1], right[HALF:])
            ).astype(BF16)
            for h in range(2):
                rows = pl.ds(h * HALF, HALF)
                left_copy(h).wait_recv()
                update_ref[rows] = dot(left_in[phase, rows], mixed)
            right_copy.wait_send()

        update = update_ref[...]
        norm = jnp.sum(update * update, keepdims=True)
        norm_out[phase] = jnp.broadcast_to(norm, (8, 128))
        norm_copy = pltpu.make_async_remote_copy(
            src_ref=norm_out.at[phase],
            dst_ref=norm_in.at[phase],
            send_sem=norm_send.at[phase],
            recv_sem=norm_recv.at[phase],
            device_id=(y, me, other),
            device_id_type=MESH,
        )
        norm_copy.start()
        norm_copy.wait()
        total = norm + norm_in[phase][0:1, 0:1]
        scale = jnp.sqrt(grad_squares) / jnp.sqrt(total + 1e-06)
        stage[phase] = (update_ref[...] * scale).astype(BF16)
        place = y if phase == 0 else n_data + lax.div(y, 2)
        for step in range(1, n_data):
            to = lax.rem(y + step, n_data)
            pltpu.make_async_remote_copy(
                src_ref=stage.at[phase, pl.ds(to * share, share)],
                dst_ref=out_ref.at[place],
                send_sem=back_send.at[phase],
                recv_sem=back_recv.at[phase],
                device_id=(to, me, r),
                device_id_type=MESH,
            ).start()
        pltpu.make_async_copy(
            stage.at[phase, pl.ds(y * share, share)], out_ref.at[place], back_recv.at[phase]
        ).start()

    has_tail = parity == y_parity

    ring_start(0)
    load.wait()
    ring_steps(0)
    ring_start(1)
    finish(0)
    ring_steps(1)
    finish(1)
    precondition(0)

    @pl.when(has_tail)
    def _():
        precondition(1)

    for phase in range(2):
        sent = rings[phase].at[pl.ds(0, 7)]
        pltpu.make_async_copy(sent, sent, ring_send.at[phase]).wait()
    sent = sums_main.at[pl.ds(0, n_owners - 1)]
    pltpu.make_async_copy(sent, sent, owner_send.at[0]).wait()

    @pl.when(has_tail)
    def _():
        sent = sums_tail.at[pl.ds(0, lead - 1)]
        pltpu.make_async_copy(sent, sent, owner_send.at[1]).wait()
        sent = stage.at[1, pl.ds(0, BS - share)]
        pltpu.make_async_copy(sent, sent, back_send.at[1]).wait()

    @pl.when(jnp.logical_not(has_tail))
    def _():
        pltpu.make_async_copy(sums_tail, sums_tail, owner_send.at[1]).wait()

    sent = stage.at[0, pl.ds(0, BS - share)]
    pltpu.make_async_copy(sent, sent, back_send.at[0]).wait()
    main_out = out_ref.at[pl.ds(0, n_data)]
    pltpu.make_async_copy(main_out, main_out, back_recv.at[0]).wait()
    tail_out = out_ref.at[pl.ds(n_data, n_data // 2)]
    pltpu.make_async_copy(tail_out, tail_out, back_recv.at[1]).wait()


def solution(mesh):
    n_data, n_owners = mesh.shape["dp"], mesh.shape["owner"]

    def on_device(gradients):
        blocks, row_part, half = gradients.shape[1:]
        slots = blocks // n_owners
        lead = n_owners // 2
        share = BS // n_data
        grouped = gradients.reshape(lead, 2, slots, row_part, half)
        vmem = pltpu.VMEM
        dma = pltpu.SemaphoreType.DMA
        return pl.pallas_call(
            functools.partial(kernel, n_data, n_owners),
            out_shape=jax.ShapeDtypeStruct((slots, share, half), BF16),
            in_specs=[pl.BlockSpec(memory_space=pl.ANY)],
            out_specs=pl.BlockSpec(memory_space=pl.ANY),
            scratch_shapes=[
                vmem((lead, 2, slots, row_part, half), BF16),
                vmem((8, lead, 2, row_part, half), BF16),
                vmem((8, lead, row_part, half), BF16),
                vmem((n_owners, row_part, half), BF16),
                vmem((lead, row_part, half), BF16),
                vmem((2, 2, BS, half), BF16),
                vmem((BS, BS), BF16),
                vmem((BS, BS), BF16),
                vmem((BS, BS), BF16),
                vmem((2, BS, BS), BF16),
                vmem((2, BS, BS), BF16),
                vmem((2, BS, half), BF16),
                vmem((2, BS, half), BF16),
                vmem((BS, half), F32),
                vmem((2, 8, 128), F32),
                vmem((2, 8, 128), F32),
                vmem((2, BS, half), BF16),
                dma,
                dma((2,)),
                dma((2, 8, 4)),
                dma((2,)),
                dma((2,)),
                dma((2,)),
                dma((2,)),
                dma((2, 2)),
                dma((2, 2)),
                dma((2,)),
                dma((2,)),
                dma((2,)),
                dma((2,)),
            ],
            compiler_params=pltpu.CompilerParams(
                collective_id=0, has_side_effects=True, vmem_limit_bytes=48 * 1024 * 1024
            ),
            name="refresh",
        )(grouped)

    return jax.shard_map(
        on_device,
        mesh=mesh,
        in_specs=(P("dp", None, "owner", "rep"),),
        out_specs=P("owner", "dp", "rep"),
        check_vma=False,
    )
```

time: 299 us -> 74.6 us (0.25)
  blocking collectives: 225 us -> 0 us
  Pallas kernels: 0 us -> 71.8 us
  waiting for transfers between devices: 28.2 us -> 0 us
  between operations: 13.5 us -> 0.01 us
  matrix products: 9.51 us -> 0 us
  other arithmetic: 7.24 us -> 0 us
  starting transfers between devices: 5.52 us -> 0 us
  local copies, waits for them, and re-layouts: 7.72 us -> 2.64 us
    all_to_all x3 -> x0, blocking collectives: 222 us -> none  [the longest x1 105 us: on_device(): lax.all_to_all(lax.all_to_all(arranged, 'dp', split_axis=1, concat_axis=1...]
    pallas_call x0 -> x1, Pallas kernels: none -> 71.8 us  [on_device(): pl.pallas_call(functools.partial(kernel, n_data, n_owners), out_shape=jax...]
    all_gather x1 -> x0, waiting for transfers between devices: 16.3 us -> none  [on_device(): whole = lax.all_gather(halves, 'rep', axis=2, tiled=True)]
    all_to_all x1 -> x0, waiting for transfers between devices: 9.67 us -> none  [on_device(): lax.all_to_all(main_final.reshape(n_data, row_share, half), 'dp', split_a...]
    dot_general x4 -> x0, matrix products: 9.51 us -> none  [the longest x2 6.37 us: mat_prod(): return jnp.dot(left, right, preferred_element_type=jnp.float32)]
    reduce_sum x2 -> x0, other arithmetic: 3.56 us -> none  [the longest x1 3.17 us: on_device(): jnp.sum(moved.astype(jnp.float32), axis=(0, 1)).astype(jnp.bfloat16)]
    all_to_all x1 -> x0, starting transfers between devices: 3.41 us -> none  [on_device(): lax.all_to_all(main_final.reshape(n_data, row_share, half), 'dp', split_a...]
  transfers between devices with their start and end apart: 3 -> 0, of which waited for: 3 -> 0; matrix products, arithmetic and copies ran while one was open for 0% -> 0% of each run, Pallas kernels for 0% -> 0%
where the time goes in v1:
time: 74.6 us; the launch traced here: 74.4 us
  Pallas kernels  71.8 us (96%)
  local copies, waits for them, and re-layouts  2.64 us (4%)
    pallas_call x1, Pallas kernels, on_device(): pl.pallas_call(functools.partial(kernel, n_data, n_owners), out_shape=jax...  71.8 us
    unnamed x3, local copies, waits for them, and re-layouts  2.64 us

profile of v1, /device:TPU:1, one launch (start us, length us, event | category | flops | bytes accessed | tf_op | source)
XLA Modules:
  0.0 74.4 jit_solution(16586395064561978454)
XLA Ops:
  0.0 0.0 copy-start
  0.0 1.9 %copy-done = bf16[1,384,16,256]{3,2,1,0:T(8,128)(2,1)S(1)} copy-done((bf16[1,384,16,256]{3,2,1,0:T(8,128)(2,1)S(1)}, bf16[1,384,16,256]{3,2,1,0:T(8,128)(2,1)}, u32[]{:S(2)}) %copy-start) | copy-done | bytes 3145752
  1.9 71.8 %refresh.1 = bf16[12,64,256]{2,1,0:T(8,128)(2,1)S(1)} custom-call(bf16[16,2,12,16,256]{4,3,2,1,0:T(8,128)(2,1)S(1)} %bitcast.1), custom_call_target="tpu_custom_call" | custom-call | tf_op jit(solution)/shard_map/refresh/pallas_call | solution.py:349
  73.7 0.7 %copy.3 = bf16[12,64,256]{2,1,0:T(8,128)(2,1)} copy(bf16[12,64,256]{2,1,0:T(8,128)(2,1)S(1)} %refresh.1) | data formatting | bytes 786432
Async XLA Ops:
  0.0 1.9 %copy-start = (bf16[1,384,16,256]{3,2,1,0:T(8,128)(2,1)S(1)}, bf16[1,384,16,256]{3,2,1,0:T(8,128)(2,1)}, u32[]{:S(2)}) copy-start(bf16[1,384,16,256]{3,2,1,0:T(8,128)(2,1)} %param.1) | copy-start | bytes 9437188

commit v2 on v1

v2 whole, which is shorter than its diff:
```python
import functools

import jax
import jax.numpy as jnp
from jax import lax
from jax.experimental import pallas as pl
from jax.experimental.pallas import tpu as pltpu
from jax.sharding import PartitionSpec as P

MESH = pl.DeviceIdType.MESH
BS = 512
HALF = BS // 2
CHUNK = 128
F32 = jnp.float32
BF16 = jnp.bfloat16


def dot(a, b):
    return jnp.dot(a, b, preferred_element_type=F32)


def dot_nt(a, b):
    return lax.dot_general(a, b, (((1,), (1,)), ((), ())), preferred_element_type=F32)


def total_of(x):
    return jnp.sum(x, keepdims=True)


def kernel(
    n_data,
    n_owners,
    g_ref,
    out_ref,
    scale_ref,
    own,
    ring_main,
    ring_tail,
    sums_main,
    sums_tail,
    gathered,
    side,
    factor_ref,
    square_ref,
    cross_ref,
    power_ref,
    left_ref,
    left_in,
    right_in,
    right_half,
    right_own,
    mixed_ref,
    norm_out,
    norm_in,
    scale_out,
    stage,
    load_sem,
    ring_send,
    ring_recv,
    owner_send,
    owner_recv,
    half_send,
    half_recv,
    left_send,
    left_recv,
    right_send,
    right_recv,
    norm_send,
    norm_recv,
    back_send,
    back_recv,
    scale_send,
    scale_recv,
    round_sem,
):
    y = lax.axis_index("dp")
    me = lax.axis_index("owner")
    r = lax.axis_index("rep")
    y_parity = lax.rem(y, 2)
    has_tail = lax.rem(me, 2) == y_parity
    other = 1 - r
    subs = 4
    lead = n_owners // 2
    part = lead // subs
    row_part = BS // n_owners
    share = BS // n_data

    load = pltpu.make_async_copy(g_ref, own, load_sem)
    load.start()

    barrier = pltpu.get_barrier_semaphore()

    def owner_at(distance):
        return lax.rem(me + (distance + n_owners), n_owners)

    neighbours = (lax.rem(y + 1, n_data), lax.rem(y + n_data - 1, n_data))
    for to in neighbours:
        pl.semaphore_signal(barrier, inc=1, device_id=(to, me, r), device_id_type=MESH)
    for distance in (1, -1):
        pl.semaphore_signal(
            barrier, inc=1, device_id=(y, owner_at(distance), r), device_id_type=MESH
        )
    pl.semaphore_signal(barrier, inc=1, device_id=(y, me, other), device_id_type=MESH)
    pl.semaphore_wait(barrier, 5)

    def round_signal(i):
        for distance in (2**i, -(2**i)):
            pl.semaphore_signal(
                round_sem.at[i],
                inc=1,
                device_id=(y, owner_at(distance), r),
                device_id_type=MESH,
            )

    def round_wait(i):
        pl.semaphore_wait(round_sem.at[i], 2)

    rings = (ring_main, ring_tail)
    sums = (sums_main, sums_tail)

    def lead_of(c):
        return lax.rem(me + c, subs) * part

    def block_part(ref, phase, dest, c):
        lead_part = pl.ds(lead_of(c), part)
        if phase == 0:
            return ref.at[lead_part, :, dest]
        return ref.at[lead_part, lax.rem(dest, 2), n_data + lax.div(dest, 2)]

    def dest_of(way, step):
        ahead = 4 - step if way == 0 else 4 + step
        return lax.rem(y + ahead, n_data)

    def ring_slot(phase, way, step, c):
        return rings[phase].at[way * 4 + step, pl.ds(c * part, part)]

    def ring_copy(phase, way, step, c, raw):
        if raw:
            source = block_part(g_ref, phase, dest_of(way, step), c)
        else:
            source = ring_slot(phase, way, step - 1, c)
        return pltpu.make_async_remote_copy(
            src_ref=source,
            dst_ref=ring_slot(phase, way, step, c),
            send_sem=ring_send.at[phase],
            recv_sem=ring_recv.at[phase, way * 4 + step, c],
            device_id=(neighbours[way], me, r),
            device_id_type=MESH,
        )

    def ring_wait(phase, way, step, c):
        slot = ring_slot(phase, way, step, c)
        pltpu.make_async_copy(slot, slot, ring_recv.at[phase, way * 4 + step, c]).wait()

    long = ((0, 1), (2, 3))
    short = ((2, 3), (0, 1))

    def ring_start(phase):
        for step, parts in ((0, long), (1, short)):
            for j in range(2):
                for way in range(2):
                    ring_copy(phase, way, step, parts[way][j], True).start()

    def ring_step(phase, way, step, c):
        ring_wait(phase, way, step, c)
        slot = ring_slot(phase, way, step, c)
        slot[...] = slot[...] + block_part(own, phase, dest_of(way, step + 1), c)[...]
        ring_copy(phase, way, step + 1, c, False).start()

    def ring_steps(phase, step):
        for j in range(2 if step == 0 else 4):
            for way in range(2):
                (a, b), (c, d) = long[way], short[way]
                order = ((a, b), (c, d, a, b), (c, a, d, b))[step]
                ring_step(phase, way, step, order[j])

    def to_owner(phase, i, k):
        source = sums[phase].at[i]
        target = gathered.at[phase, r, pl.ds(me * row_part, row_part)]
        arrived = owner_recv.at[phase, lax.div(me, n_owners // 2)]

        @pl.when(k != me)
        def _():
            pltpu.make_async_remote_copy(
                src_ref=source,
                dst_ref=target,
                send_sem=owner_send.at[phase],
                recv_sem=arrived,
                device_id=(y, k, r),
                device_id_type=MESH,
            ).start()

        @pl.when(k == me)
        def _():
            pltpu.make_async_copy(source, target, arrived).start()

    def finish(phase):
        for c in (2, 0, 3, 1):
            for way in range(2):
                ring_wait(phase, way, 3, c)
            total = (
                ring_slot(phase, 0, 3, c)[...].astype(F32)
                + ring_slot(phase, 1, 3, c)[...].astype(F32)
                + block_part(own, phase, y, c)[...].astype(F32)
            ).astype(BF16)
            count = part * (2 if phase == 0 else 1)
            first = lax.rem(me + c, subs) * count
            sums[phase][pl.ds(first, count)] = total.reshape(count, row_part, HALF)

            @pl.loop(0, count)
            def _(i):
                at = first + lax.rem(i + lax.div(me, subs), count)
                k = at if phase == 0 else 2 * at + y_parity
                to_owner(phase, at, k)

    def to_core(source, target, send_sem, recv_sem):
        return pltpu.make_async_remote_copy(
            src_ref=source,
            dst_ref=target,
            send_sem=send_sem,
            recv_sem=recv_sem,
            device_id=(y, me, other),
            device_id_type=MESH,
        )

    eye = (
        lax.broadcasted_iota(jnp.int32, (CHUNK, CHUNK), 0)
        == lax.broadcasted_iota(jnp.int32, (CHUNK, CHUNK), 1)
    ).astype(F32)

    def row_chunk(j):
        chunk = lax.rem(lax.div(y, 2) + (2, 3, 1, 0)[j], BS // CHUNK)
        return chunk, pl.ds(pl.multiple_of(chunk * CHUNK, CHUNK), CHUNK)

    def precondition(phase):
        def swap(h):
            rows = gathered.at[phase, r, pl.ds(h * HALF, HALF)]
            return to_core(rows, rows, half_send.at[phase, h], half_recv.at[phase, h])

        for h in range(2):
            rows = gathered.at[phase, r, pl.ds(h * HALF, HALF)]
            pltpu.make_async_copy(rows, rows, owner_recv.at[phase, h]).wait()
            swap(h).start()
        half = gathered[phase, r]
        grad_squares = total_of(jnp.square(half.astype(F32)))

        @pl.when(r == 0)
        def _():
            side[:, :HALF] = gathered[phase, 0]

        @pl.when(r == 1)
        def _():
            side[HALF:, :] = gathered[phase, 1].T

        for h in range(2):
            swap(h).wait()

        @pl.when(r == 0)
        def _():
            side[:, HALF:] = gathered[phase, 1]

        @pl.when(r == 1)
        def _():
            side[:HALF, :] = gathered[phase, 0].T

        squares = jnp.zeros((1, 1), F32)
        for i in range(2):
            rows = pl.ds(i * HALF, HALF)
            factor = dot_nt(side[rows, :], side[...])
            squares = squares + total_of(factor * factor)
            factor_ref[rows, :] = factor.astype(BF16)
        sa = 0.5 / jnp.sqrt(squares + 1e-06)
        for i in range(2):
            rows = pl.ds(i * HALF, HALF)
            a = factor_ref[rows, :].astype(F32) * sa
            a_square = dot(factor_ref[rows, :], factor_ref[...]) * sa * sa
            cross_ref[rows, :] = (a - a_square).astype(BF16)
            square = a_square - 2.0 * a
            square_ref[rows, :] = square.astype(BF16)
            for j in range(HALF // CHUNK):
                at = i * HALF + j * CHUNK
                spot = pl.ds(at, CHUNK)
                square_ref[spot, spot] = (
                    square[j * CHUNK : (j + 1) * CHUNK, at : at + CHUNK] + eye
                ).astype(BF16)
        for i in range(2):
            rows = pl.ds(i * HALF, HALF)
            power_ref[rows, :] = dot(square_ref[rows, :], square_ref[...]).astype(BF16)

        def root_part(rows, start, cols):
            a = factor_ref[rows, cols].astype(F32) * (sa * 1.5625)
            value = dot(cross_ref[rows, :], power_ref[:, cols]) * (-(1.25**6)) - a
            row = lax.broadcasted_iota(jnp.int32, value.shape, 0) + start
            col = lax.broadcasted_iota(jnp.int32, value.shape, 1) + (cols.start or 0)
            return jnp.where(row == col, value + 1.5625, value).astype(BF16)

        def left_copy(j):
            _, rows = row_chunk(j)
            return to_core(
                left_ref.at[phase, rows],
                left_in.at[phase, rows],
                left_send.at[phase, j],
                left_recv.at[phase, j],
            )

        right_copy = to_core(
            right_half.at[phase], right_in.at[phase], right_send.at[phase], right_recv.at[phase]
        )
        place = y if phase == 0 else n_data + lax.div(y, 2)

        def send_back(j, update):
            chunk, rows = row_chunk(j)
            stage[phase, rows] = update.astype(BF16)
            for half in range(2):
                to = chunk * 2 + half
                source = stage.at[phase, pl.ds(pl.multiple_of(to * share, share), share)]

                @pl.when(to != y)
                def _():
                    pltpu.make_async_remote_copy(
                        src_ref=source,
                        dst_ref=out_ref.at[place],
                        send_sem=back_send.at[phase],
                        recv_sem=back_recv.at[phase],
                        device_id=(to, me, r),
                        device_id_type=MESH,
                    ).start()

                @pl.when(to == y)
                def _():
                    pltpu.make_async_copy(
                        source, out_ref.at[place], back_recv.at[phase]
                    ).start()

        def put_norm(norm):
            norm_out[phase, 0:4] = jnp.broadcast_to(norm, (4, 128))

        norm_out[phase, 4:8] = jnp.broadcast_to(grad_squares, (4, 128))

        @pl.when(r == 0)
        def _():
            for j in range(BS // CHUNK):
                chunk, rows = row_chunk(j)
                left_ref[phase, rows] = root_part(rows, chunk * CHUNK, slice(0, BS))
                left_copy(j).start()
            for j in range(BS // CHUNK):
                _, rows = row_chunk(j)
                mixed_ref[rows] = dot(left_ref[phase, rows], side[...]).astype(BF16)
            right_copy.wait_recv()
            norm = jnp.zeros((1, 1), F32)
            for j in range(BS // CHUNK):
                _, rows = row_chunk(j)
                update = dot(mixed_ref[rows], right_in[phase])
                send_back(j, update)
                norm = norm + total_of(update * update)
            put_norm(norm)
            for j in range(BS // CHUNK):
                left_copy(j).wait_send()

        @pl.when(r == 1)
        def _():
            for i in range(2):
                rows = pl.ds(i * HALF, HALF)
                right_half[phase, rows] = root_part(rows, i * HALF, slice(0, HALF))
            right_copy.start()
            for i in range(2):
                rows = pl.ds(i * HALF, HALF)
                right_own[rows] = root_part(rows, i * HALF, slice(HALF, BS))
            for i in range(2):
                rows = pl.ds(i * HALF, HALF)
                mixed_ref[rows, :HALF] = (
                    dot(gathered[phase, 0, rows], right_own[:HALF])
                    + dot(gathered[phase, 1, rows], right_own[HALF:])
                ).astype(BF16)
            norm = jnp.zeros((1, 1), F32)
            for j in range(BS // CHUNK):
                _, rows = row_chunk(j)
                left_copy(j).wait_recv()
                update = dot(left_in[phase, rows], mixed_ref[:, :HALF])
                send_back(j, update)
                norm = norm + total_of(update * update)
            put_norm(norm)
            right_copy.wait_send()

        norm_copy = to_core(
            norm_out.at[phase], norm_in.at[phase], norm_send.at[phase], norm_recv.at[phase]
        )
        norm_copy.start()
        norm_copy.wait()
        both = norm_out[phase] + norm_in[phase]
        scale = jnp.sqrt(both[4:5]) / jnp.sqrt(both[0:1] + 1e-06)
        scale_out[phase] = jnp.broadcast_to(scale, (8, 128))
        for distance in (4, 3, 5, 2, 6, 1, 7):
            pltpu.make_async_remote_copy(
                src_ref=scale_out.at[phase],
                dst_ref=scale_ref.at[place],
                send_sem=scale_send.at[phase],
                recv_sem=scale_recv.at[phase],
                device_id=(lax.rem(y + distance, n_data), me, r),
                device_id_type=MESH,
            ).start()
        pltpu.make_async_copy(
            scale_out.at[phase], scale_ref.at[place], scale_recv.at[phase]
        ).start()

    ring_start(0)
    round_signal(0)
    load.wait()
    ring_steps(0, 0)
    for i in range(3):
        round_wait(i)
        round_signal(i + 1)
        if i < 2:
            ring_steps(0, i + 1)
    ring_start(1)
    round_wait(3)
    finish(0)
    for step in range(3):
        ring_steps(1, step)
    finish(1)
    precondition(0)

    @pl.when(has_tail)
    def _():
        precondition(1)

    def wait_for(ref, sem):
        pltpu.make_async_copy(ref, ref, sem).wait()

    for phase in range(2):
        wait_for(rings[phase].at[pl.ds(0, 7)], ring_send.at[phase])
    wait_for(sums_main.at[pl.ds(0, n_owners - 1)], owner_send.at[0])
    wait_for(stage.at[0, pl.ds(0, BS - share)], back_send.at[0])
    wait_for(scale_ref.at[pl.ds(0, n_data - 1)], scale_send.at[0])

    @pl.when(has_tail)
    def _():
        wait_for(sums_tail.at[pl.ds(0, lead - 1)], owner_send.at[1])
        wait_for(stage.at[1, pl.ds(0, BS - share)], back_send.at[1])
        wait_for(scale_ref.at[pl.ds(0, n_data - 1)], scale_send.at[1])

    @pl.when(jnp.logical_not(has_tail))
    def _():
        wait_for(sums_tail, owner_send.at[1])

    for phase, first, count in ((0, 0, n_data), (1, n_data, n_data // 2)):
        places = pl.ds(first, count)
        wait_for(out_ref.at[places], back_recv.at[phase])
        wait_for(scale_ref.at[places], scale_recv.at[phase])


def solution(mesh):
    n_data, n_owners = mesh.shape["dp"], mesh.shape["owner"]

    def on_device(gradients):
        blocks, row_part, half = gradients.shape[1:]
        slots = blocks // n_owners
        lead = n_owners // 2
        share = BS // n_data
        grouped = gradients.reshape(lead, 2, slots, row_part, half)
        vmem = pltpu.VMEM
        dma = pltpu.SemaphoreType.DMA
        pieces, scales = pl.pallas_call(
            functools.partial(kernel, n_data, n_owners),
            out_shape=(
                jax.ShapeDtypeStruct((slots, share, half), BF16),
                jax.ShapeDtypeStruct((slots, 8, 128), F32),
            ),
            in_specs=[pl.BlockSpec(memory_space=pltpu.HBM)],
            out_specs=[pl.BlockSpec(memory_space=pl.ANY)] * 2,
            scratch_shapes=[
                vmem((lead, 2, slots, row_part, half), BF16),
                vmem((8, lead, 2, row_part, half), BF16),
                vmem((8, lead, row_part, half), BF16),
                vmem((n_owners, row_part, half), BF16),
                vmem((lead, row_part, half), BF16),
                vmem((2, 2, BS, half), BF16),
                vmem((BS, BS), BF16),
                vmem((BS, BS), BF16),
                vmem((BS, BS), BF16),
                vmem((BS, BS), BF16),
                vmem((BS, BS), BF16),
                vmem((2, BS, BS), BF16),
                vmem((2, BS, BS), BF16),
                vmem((2, BS, half), BF16),
                vmem((2, BS, half), BF16),
                vmem((BS, half), BF16),
                vmem((BS, BS), BF16),
                vmem((2, 8, 128), F32),
                vmem((2, 8, 128), F32),
                vmem((2, 8, 128), F32),
                vmem((2, BS, half), BF16),
                dma,
                dma((2,)),
                dma((2, 8, 4)),
                dma((2,)),
                dma((2, 2)),
                dma((2, 2)),
                dma((2, 2)),
                dma((2, 4)),
                dma((2, 4)),
                dma((2,)),
                dma((2,)),
                dma((2,)),
                dma((2,)),
                dma((2,)),
                dma((2,)),
                dma((2,)),
                dma((2,)),
                pltpu.SemaphoreType.REGULAR((4,)),
            ],
            compiler_params=pltpu.CompilerParams(
                collective_id=0, has_side_effects=True, vmem_limit_bytes=52 * 1024 * 1024
            ),
            name="refresh",
        )(grouped)
        return (pieces.astype(F32) * scales[:, :1, :1]).astype(BF16)

    return jax.shard_map(
        on_device,
        mesh=mesh,
        in_specs=(P("dp", None, "owner", "rep"),),
        out_specs=P("owner", "dp", "rep"),
        check_vma=False,
    )
```

time: 74.6 us -> 71.5 us (0.958)
  local copies, waits for them, and re-layouts: 2.64 us -> 0.17 us
  Pallas kernels: 71.8 us -> 70.3 us
  other arithmetic: 0 us -> 0.88 us
    unnamed x3 -> x0, local copies, waits for them, and re-layouts: 2.64 us -> none
    pallas_call x1, Pallas kernels: 71.8 us -> 70.3 us  [on_device(): pl.pallas_call(functools.partial(kernel, n_data, n_owners), out_shape=(ja...]
    convert_element_type x0 -> x1, other arithmetic: none -> 0.88 us  [on_device(): return (pieces.astype(F32) * scales[:, :1, :1]).astype(BF16)]
where the time goes in v2:
time: 71.5 us; the launch traced here: 71.4 us
  Pallas kernels  70.3 us (98%)
  other arithmetic  0.88 us (1%)
    pallas_call x1, Pallas kernels, on_device(): pl.pallas_call(functools.partial(kernel, n_data, n_owners), out_shape=(ja...  70.3 us

profile of v2, /device:TPU:1, one launch (start us, length us, event | category | flops | bytes accessed | tf_op | source)
XLA Modules:
  0.0 71.4 jit_solution(8272982464392954531)
XLA Ops:
  0.0 70.3 %refresh.1 = (bf16[12,64,256]{2,1,0:T(8,128)(2,1)S(1)}, f32[12,8,128]{2,1,0:T(8,128)S(1)}) custom-call(bf16[16,2,12,16,256]{4,3,2,1,0:T(8,128)(2,1)} %bitcast.1), custom_call_target="tpu_custom_call" | custom-call | tf_op jit(solution)/shard_map/refresh/pallas_call | solution.py:463
  70.3 0.2 slice_reduce_fusion
  70.5 0.9 %multiply_convert_fusion = bf16[12,64,256]{2,1,0:T(8,128)(2,1)} fusion(bf16[12,64,256]{2,1,0:T(8,128)(2,1)S(1)} %get-tuple-element.7, f32[12]{0:T(128)S(1)} %slice_reduce_fusion), kind=kLoop, calls=%fused_computation | loop fusion | flops 589824 | bytes 786480 | tf_op jit(solution)/shard_map/convert_element_type | solution.py:517

commit v3 on v2

v3 whole, which is shorter than its diff:
```python
import functools

import jax
import jax.numpy as jnp
from jax import lax
from jax.experimental import pallas as pl
from jax.experimental.pallas import tpu as pltpu
from jax.sharding import PartitionSpec as P

MESH = pl.DeviceIdType.MESH
BS = 512
HALF = BS // 2
CHUNK = 128
F32 = jnp.float32
BF16 = jnp.bfloat16


def dot(a, b):
    return jnp.dot(a, b, preferred_element_type=F32)


def dot_nt(a, b):
    return lax.dot_general(a, b, (((1,), (1,)), ((), ())), preferred_element_type=F32)


def total_of(x):
    return jnp.sum(x, keepdims=True)


def kernel(
    n_data,
    n_owners,
    g_ref,
    out_ref,
    own,
    ring_main,
    ring_tail,
    sums_main,
    sums_tail,
    gathered,
    side,
    factor_ref,
    square_ref,
    cross_ref,
    power_ref,
    left_ref,
    left_in,
    right_in,
    right_ref,
    mixed_ref,
    partial_ref,
    sums_ref,
    update_ref,
    stage,
    load_sem,
    ring_send,
    ring_recv,
    owner_send,
    owner_recv,
    half_send,
    half_recv,
    left_send,
    left_recv,
    right_send,
    right_recv,
    back_send,
    back_recv,
    round_sem,
):
    y = lax.axis_index("dp")
    me = lax.axis_index("owner")
    r = lax.axis_index("rep")
    y_parity = lax.rem(y, 2)
    has_tail = lax.rem(me, 2) == y_parity
    other = 1 - r
    subs = 4
    lead = n_owners // 2
    part = lead // subs
    row_part = BS // n_owners
    share = BS // n_data

    load = pltpu.make_async_copy(g_ref, own, load_sem)
    load.start()

    barrier = pltpu.get_barrier_semaphore()

    def owner_at(distance):
        return lax.rem(me + (distance + n_owners), n_owners)

    neighbours = (lax.rem(y + 1, n_data), lax.rem(y + n_data - 1, n_data))
    for to in neighbours:
        pl.semaphore_signal(barrier, inc=1, device_id=(to, me, r), device_id_type=MESH)
    for distance in (1, -1):
        pl.semaphore_signal(
            barrier, inc=1, device_id=(y, owner_at(distance), r), device_id_type=MESH
        )
    pl.semaphore_signal(barrier, inc=1, device_id=(y, me, other), device_id_type=MESH)
    pl.semaphore_wait(barrier, 5)

    def round_signal(i):
        for distance in (2**i, -(2**i)):
            pl.semaphore_signal(
                round_sem.at[i],
                inc=1,
                device_id=(y, owner_at(distance), r),
                device_id_type=MESH,
            )

    def round_wait(i):
        pl.semaphore_wait(round_sem.at[i], 2)

    rings = (ring_main, ring_tail)
    sums = (sums_main, sums_tail)

    planes = (1, 0, 2, 3)
    plane_size = n_owners // subs
    my_plane = lax.div(me, plane_size)
    my_z = lax.rem(me, plane_size)

    def plane_of(c):
        return lax.rem(my_plane + planes[c], subs)

    def lead_of(c):
        return plane_of(c) * part

    def block_part(ref, phase, dest, c):
        lead_part = pl.ds(lead_of(c), part)
        if phase == 0:
            return ref.at[lead_part, :, dest]
        return ref.at[lead_part, lax.rem(dest, 2), n_data + lax.div(dest, 2)]

    def dest_of(way, step):
        ahead = 4 - step if way == 0 else 4 + step
        return lax.rem(y + ahead, n_data)

    def ring_slot(phase, way, step, c):
        return rings[phase].at[way * 4 + step, pl.ds(c * part, part)]

    def ring_copy(phase, way, step, c, raw):
        if raw:
            source = block_part(g_ref, phase, dest_of(way, step), c)
        else:
            source = ring_slot(phase, way, step - 1, c)
        return pltpu.make_async_remote_copy(
            src_ref=source,
            dst_ref=ring_slot(phase, way, step, c),
            send_sem=ring_send.at[phase],
            recv_sem=ring_recv.at[phase, way * 4 + step, c],
            device_id=(neighbours[way], me, r),
            device_id_type=MESH,
        )

    def ring_wait(phase, way, step, c):
        slot = ring_slot(phase, way, step, c)
        pltpu.make_async_copy(slot, slot, ring_recv.at[phase, way * 4 + step, c]).wait()

    long = ((0, 1), (2, 3))
    short = ((2, 3), (0, 1))

    def ring_start(phase, step, j):
        parts = (long, short)[step]
        for way in range(2):
            ring_copy(phase, way, step, parts[way][j], True).start()

    def ring_step(phase, way, step, c):
        ring_wait(phase, way, step, c)
        slot = ring_slot(phase, way, step, c)
        slot[...] = slot[...] + block_part(own, phase, dest_of(way, step + 1), c)[...]
        ring_copy(phase, way, step + 1, c, False).start()

    def ring_steps(phase, step, j):
        for way in range(2):
            (a, b), (c, d) = long[way], short[way]
            order = ((a, b), (c, d, a, b), (c, a, d, b))[step]
            ring_step(phase, way, step, order[j])

    def to_owner(phase, i, k, local):
        source = sums[phase].at[i]
        target = gathered.at[phase, r, pl.ds(me * row_part, row_part)]
        arrived = owner_recv.at[phase, lax.div(me, n_owners // 2)]
        if local:
            pltpu.make_async_copy(source, target, arrived).start()
        else:
            pltpu.make_async_remote_copy(
                src_ref=source,
                dst_ref=target,
                send_sem=owner_send.at[phase],
                recv_sem=arrived,
                device_id=(y, k, r),
                device_id_type=MESH,
            ).start()

    def finish(phase, c):
        for way in range(2):
            ring_wait(phase, way, 3, c)
        total = (
            ring_slot(phase, 0, 3, c)[...].astype(F32)
            + ring_slot(phase, 1, 3, c)[...].astype(F32)
            + block_part(own, phase, y, c)[...].astype(F32)
        ).astype(BF16)
        count = part * (2 if phase == 0 else 1)
        plane = plane_of(c)
        sums[phase][pl.ds(plane * count, count)] = total.reshape(count, row_part, HALF)
        if phase == 0:
            for distance in (4, 3, 5, 2, 6, 1, 7, 0):
                k = plane * plane_size + lax.rem(my_z + distance, plane_size)
                to_owner(0, k, k, distance == 0 and planes[c] == 0)
        else:
            for distance in (4, 2, 6, 0):
                z = lax.rem(my_z + distance + jnp.where(has_tail, 0, 1), plane_size)
                i = plane * count + lax.div(z, 2)
                k = plane * plane_size + z
                if distance == 0 and planes[c] == 0:

                    @pl.when(has_tail)
                    def _():
                        to_owner(1, i, k, True)

                    @pl.when(jnp.logical_not(has_tail))
                    def _():
                        to_owner(1, i, k, False)

                else:
                    to_owner(1, i, k, False)

    def to_core(source, target, send_sem, recv_sem):
        return pltpu.make_async_remote_copy(
            src_ref=source,
            dst_ref=target,
            send_sem=send_sem,
            recv_sem=recv_sem,
            device_id=(y, me, other),
            device_id_type=MESH,
        )

    eye = (
        lax.broadcasted_iota(jnp.int32, (CHUNK, CHUNK), 0)
        == lax.broadcasted_iota(jnp.int32, (CHUNK, CHUNK), 1)
    ).astype(F32)

    def swap(phase, h):
        rows = gathered.at[phase, r, pl.ds(h * HALF, HALF)]
        return to_core(rows, rows, half_send.at[phase, h], half_recv.at[phase, h])

    def gather(phase):
        for h in range(2):
            rows = gathered.at[phase, r, pl.ds(h * HALF, HALF)]
            pltpu.make_async_copy(rows, rows, owner_recv.at[phase, h]).wait()
            swap(phase, h).start()
        @pl.when(r == 0)
        def _():
            own_half = gathered[phase, 0]
            partial_ref[...] = dot_nt(own_half, own_half)

        @pl.when(r == 1)
        def _():
            side[HALF:, :] = gathered[phase, 1].T
            partial_ref[HALF:, HALF:] = dot_nt(side[HALF:, :], side[HALF:, :])

    def precondition(phase):
        for h in range(2):
            swap(phase, h).wait()

        def keep(parts):
            squares = jnp.zeros((1, 1), F32)
            diagonal = jnp.zeros((CHUNK, CHUNK), F32)
            for row, col, value in parts:
                height, width = value.shape
                factor_ref[row : row + height, col : col + width] = value.astype(BF16)
                squares = squares + total_of(value * value)
                for at in range(max(row, col), min(row + height, col + width), CHUNK):
                    i, j = at - row, at - col
                    diagonal = diagonal + value[i : i + CHUNK, j : j + CHUNK] * eye
            sums_ref[0:8] = jnp.broadcast_to(squares, (8, 128))
            sums_ref[8:16] = jnp.broadcast_to(total_of(diagonal), (8, 128))

        @pl.when(r == 0)
        def _():
            side[:, :HALF] = gathered[phase, 0]
            side[:, HALF:] = gathered[phase, 1]
            parts = []
            for row in (0, HALF):
                rows = slice(row, row + HALF)
                parts.append(
                    (row, 0, partial_ref[rows, :] + dot_nt(side[rows, HALF:], side[:, HALF:]))
                )
            keep(parts)

        @pl.when(r == 1)
        def _():
            side[:HALF, :] = gathered[phase, 0].T
            keep(
                (
                    (0, 0, dot_nt(side[:HALF, :], side[...])),
                    (HALF, 0, dot_nt(side[HALF:, :], side[:HALF, :])),
                    (HALF, HALF, partial_ref[HALF:, HALF:]),
                )
            )

        squares = sums_ref[0:1, 0:1]
        grad_squares = sums_ref[8:9, 0:1]
        yield
        sa = 0.5 / jnp.sqrt(squares + 1e-06)
        for i in range(2):
            rows = pl.ds(i * HALF, HALF)
            a = factor_ref[rows, :].astype(F32) * sa
            a_square = dot(factor_ref[rows, :], factor_ref[...]) * sa * sa
            cross_ref[rows, :] = (a - a_square).astype(BF16)
            square = a_square - 2.0 * a
            square_ref[rows, :] = square.astype(BF16)
            for j in range(HALF // CHUNK):
                at = i * HALF + j * CHUNK
                spot = pl.ds(at, CHUNK)
                square_ref[spot, spot] = (
                    square[j * CHUNK : (j + 1) * CHUNK, at : at + CHUNK] + eye
                ).astype(BF16)
            yield
        for i in range(2):
            rows = pl.ds(i * HALF, HALF)
            power_ref[rows, :] = dot(square_ref[rows, :], square_ref[...]).astype(BF16)
        yield

        def root_part(rows, cols):
            a = factor_ref[rows, cols].astype(F32) * (sa * 1.5625)
            value = dot(cross_ref[rows, :], power_ref[:, cols]) * (-(1.25**6)) - a
            row = lax.broadcasted_iota(jnp.int32, value.shape, 0) + rows.start
            col = lax.broadcasted_iota(jnp.int32, value.shape, 1) + cols.start
            return jnp.where(row == col, value + 1.5625, value).astype(BF16)

        halves = (slice(0, HALF), slice(HALF, BS))
        chunks = [slice(i, i + CHUNK) for i in range(0, BS, CHUNK)]

        def left_copy(j):
            rows = pl.ds(j * CHUNK, CHUNK)
            return to_core(
                left_ref.at[phase, rows],
                left_in.at[phase, rows],
                left_send.at[phase, j],
                left_recv.at[phase, j],
            )

        def right_copy(h):
            return to_core(
                right_ref.at[phase, h],
                right_in.at[phase, h],
                right_send.at[phase, h],
                right_recv.at[phase, h],
            )

        def put_norm(norm):
            sums_ref[0:8] = jnp.broadcast_to(norm, (8, 128))

        @pl.when(r == 0)
        def _():
            for j, rows in enumerate(chunks):
                left_ref[phase, rows] = root_part(rows, slice(0, BS))
                left_copy(j).start()
            for rows in halves:
                mixed_ref[rows] = dot(left_ref[phase, rows], side[...]).astype(BF16)
            norm = jnp.zeros((1, 1), F32)
            for h in range(2):
                right_copy(h).wait_recv()
                for rows in halves:
                    update = dot(mixed_ref[rows], right_in[phase, h])
                    norm = norm + total_of(update * update)
                    if h == 0:
                        update_ref[rows] = update
            put_norm(norm)

        @pl.when(r == 1)
        def _():
            for h, cols in enumerate(halves):
                for rows in halves:
                    right_ref[phase, h, rows] = root_part(rows, cols)
                right_copy(h).start()
            for h, cols in enumerate(halves):
                for rows in halves:
                    mixed_ref[rows, cols] = (
                        dot(gathered[phase, 0, rows], right_ref[phase, h, halves[0]])
                        + dot(gathered[phase, 1, rows], right_ref[phase, h, halves[1]])
                    ).astype(BF16)
            norm = jnp.zeros((1, 1), F32)
            for j, rows in enumerate(chunks):
                left_copy(j).wait_recv()
                update = dot(left_in[phase, rows], mixed_ref[...])
                norm = norm + total_of(update * update)
                update_ref[rows] = update[:, HALF:]
            put_norm(norm)

        scale = jnp.sqrt(grad_squares) / jnp.sqrt(sums_ref[0:1, 0:1] + 1e-06)
        place = y if phase == 0 else n_data + lax.div(y, 2)
        yield
        for distance in (4, 3, 5, 2, 6, 1, 7, 0):
            to = lax.rem(y + distance, n_data)
            rows = pl.ds(pl.multiple_of(to * share, share), share)
            stage[phase, rows] = (update_ref[rows] * scale).astype(BF16)
            if distance:
                pltpu.make_async_remote_copy(
                    src_ref=stage.at[phase, rows],
                    dst_ref=out_ref.at[place],
                    send_sem=back_send.at[phase],
                    recv_sem=back_recv.at[phase],
                    device_id=(to, me, r),
                    device_id_type=MESH,
                ).start()
            else:
                pltpu.make_async_copy(
                    stage.at[phase, rows], out_ref.at[place], back_recv.at[phase]
                ).start()

        @pl.when(r == 0)
        def _():
            for j in range(len(chunks)):
                left_copy(j).wait_send()

        @pl.when(r == 1)
        def _():
            for h in range(2):
                right_copy(h).wait_send()

        yield

    for step in range(2):
        for j in range(2):
            ring_start(0, step, j)
    round_signal(0)
    load.wait()
    for j in range(2):
        ring_steps(0, 0, j)
    round_wait(0)
    round_signal(1)
    for j in range(4):
        ring_steps(0, 1, j)
    round_wait(1)
    round_signal(2)
    def advance(stages, count):
        for _ in range(count):
            next(stages)

    main = precondition(0)
    ring_steps(0, 2, 0)
    ring_steps(0, 2, 1)
    ring_steps(0, 2, 2)
    ring_steps(0, 2, 3)
    ring_start(1, 0, 0)
    ring_start(1, 0, 1)
    ring_start(1, 1, 0)
    ring_start(1, 1, 1)
    round_wait(2)
    round_signal(3)
    round_wait(3)
    finish(0, 2)
    finish(0, 0)
    finish(0, 3)
    finish(0, 1)
    ring_steps(1, 0, 0)
    ring_steps(1, 0, 1)
    ring_steps(1, 1, 0)
    ring_steps(1, 1, 1)
    ring_steps(1, 1, 2)
    ring_steps(1, 1, 3)
    gather(0)
    ring_steps(1, 2, 0)
    ring_steps(1, 2, 1)
    advance(main, 1)
    ring_steps(1, 2, 2)
    advance(main, 1)
    ring_steps(1, 2, 3)
    advance(main, 1)
    finish(1, 2)
    finish(1, 0)
    advance(main, 1)
    finish(1, 3)
    finish(1, 1)
    advance(main, 1)

    @pl.when(has_tail)
    def _():
        gather(1)

    advance(main, 1)

    @pl.when(has_tail)
    def _():
        advance(precondition(1), 6)

    def wait_for(ref, sem):
        pltpu.make_async_copy(ref, ref, sem).wait()

    for phase in range(2):
        wait_for(rings[phase].at[pl.ds(0, 7)], ring_send.at[phase])
    wait_for(sums_main.at[pl.ds(0, n_owners - 1)], owner_send.at[0])
    wait_for(stage.at[0, pl.ds(0, BS - share)], back_send.at[0])

    @pl.when(has_tail)
    def _():
        wait_for(sums_tail.at[pl.ds(0, lead - 1)], owner_send.at[1])
        wait_for(stage.at[1, pl.ds(0, BS - share)], back_send.at[1])

    @pl.when(jnp.logical_not(has_tail))
    def _():
        wait_for(sums_tail, owner_send.at[1])

    for phase, first, count in ((0, 0, n_data), (1, n_data, n_data // 2)):
        places = pl.ds(first, count)
        wait_for(out_ref.at[places], back_recv.at[phase])


def solution(mesh):
    n_data, n_owners = mesh.shape["dp"], mesh.shape["owner"]

    def on_device(gradients):
        blocks, row_part, half = gradients.shape[1:]
        slots = blocks // n_owners
        lead = n_owners // 2
        share = BS // n_data
        grouped = gradients.reshape(lead, 2, slots, row_part, half)
        vmem = pltpu.VMEM
        dma = pltpu.SemaphoreType.DMA
        return pl.pallas_call(
            functools.partial(kernel, n_data, n_owners),
            out_shape=jax.ShapeDtypeStruct((slots, share, half), BF16),
            in_specs=[pl.BlockSpec(memory_space=pltpu.HBM)],
            out_specs=pl.BlockSpec(memory_space=pl.ANY),
            scratch_shapes=[
                vmem((lead, 2, slots, row_part, half), BF16),
                vmem((8, lead, 2, row_part, half), BF16),
                vmem((8, lead, row_part, half), BF16),
                vmem((n_owners, row_part, half), BF16),
                vmem((lead, row_part, half), BF16),
                vmem((2, 2, BS, half), BF16),
                vmem((BS, BS), BF16),
                vmem((BS, BS), BF16),
                vmem((BS, BS), BF16),
                vmem((BS, BS), BF16),
                vmem((BS, BS), BF16),
                vmem((2, BS, BS), BF16),
                vmem((2, BS, BS), BF16),
                vmem((2, 2, BS, half), BF16),
                vmem((2, 2, BS, half), BF16),
                vmem((BS, BS), BF16),
                vmem((BS, BS), F32),
                vmem((16, 128), F32),
                vmem((BS, half), F32),
                vmem((2, BS, half), BF16),
                dma,
                dma((2,)),
                dma((2, 8, 4)),
                dma((2,)),
                dma((2, 2)),
                dma((2, 2)),
                dma((2, 2)),
                dma((2, 4)),
                dma((2, 4)),
                dma((2, 2)),
                dma((2, 2)),
                dma((2,)),
                dma((2,)),
                pltpu.SemaphoreType.REGULAR((4,)),
            ],
            compiler_params=pltpu.CompilerParams(
                collective_id=0, has_side_effects=True, vmem_limit_bytes=52 * 1024 * 1024
            ),
            name="refresh",
        )(grouped)

    return jax.shard_map(
        on_device,
        mesh=mesh,
        in_specs=(P("dp", None, "owner", "rep"),),
        out_specs=P("owner", "dp", "rep"),
        check_vma=False,
    )
```

time: 71.5 us -> 67.1 us (0.938)
  Pallas kernels: 70.3 us -> 66.2 us
  other arithmetic: 0.88 us -> 0 us
    pallas_call x1, Pallas kernels: 70.3 us -> 66.2 us  [on_device(): pl.pallas_call(functools.partial(kernel, n_data, n_owners), out_shape=jax...]
    convert_element_type x1 -> x0, other arithmetic: 0.88 us -> none  [on_device(): return (pieces.astype(F32) * scales[:, :1, :1]).astype(BF16)]
    unnamed x0 -> x1, local copies, waits for them, and re-layouts: none -> 0.75 us
where the time goes in v3:
time: 67.1 us; the launch traced here: 66.9 us
  Pallas kernels  66.2 us (99%)
  local copies, waits for them, and re-layouts  0.75 us (1%)
    pallas_call x1, Pallas kernels, on_device(): pl.pallas_call(functools.partial(kernel, n_data, n_owners), out_shape=jax...  66.2 us

profile of v3, /device:TPU:1, one launch (start us, length us, event | category | flops | bytes accessed | tf_op | source)
XLA Modules:
  0.0 66.9 jit_solution(10776251499666321777)
XLA Ops:
  0.0 66.2 %refresh.1 = bf16[12,64,256]{2,1,0:T(8,128)(2,1)S(1)} custom-call(bf16[16,2,12,16,256]{4,3,2,1,0:T(8,128)(2,1)} %bitcast.1), custom_call_target="tpu_custom_call" | custom-call | tf_op jit(solution)/shard_map/refresh/pallas_call | solution.py:520
  66.2 0.7 %copy.3 = bf16[12,64,256]{2,1,0:T(8,128)(2,1)} copy(bf16[12,64,256]{2,1,0:T(8,128)(2,1)S(1)} %refresh.1) | data formatting | bytes 786432

commit v4 on v3

--- a/solution.py
+++ b/solution.py
@@ -50,6 +50,7 @@
     mixed_ref,
     partial_ref,
     sums_ref,
+    norms_ref,
     update_ref,
     stage,
     load_sem,
@@ -318,7 +319,7 @@
         for i in range(2):
             rows = pl.ds(i * HALF, HALF)
             power_ref[rows, :] = dot(square_ref[rows, :], square_ref[...]).astype(BF16)
-        yield
+            yield
 
         def root_part(rows, cols):
             a = factor_ref[rows, cols].astype(F32) * (sa * 1.5625)
@@ -347,49 +348,64 @@
                 right_recv.at[phase, h],
             )
 
-        def put_norm(norm):
-            sums_ref[0:8] = jnp.broadcast_to(norm, (8, 128))
-
-        @pl.when(r == 0)
-        def _():
-            for j, rows in enumerate(chunks):
-                left_ref[phase, rows] = root_part(rows, slice(0, BS))
-                left_copy(j).start()
-            for rows in halves:
-                mixed_ref[rows] = dot(left_ref[phase, rows], side[...]).astype(BF16)
-            norm = jnp.zeros((1, 1), F32)
-            for h in range(2):
+        norms = norms_ref.at[phase]
+        for h, part_rows in enumerate((chunks[:2], chunks[2:])):
+
+            @pl.when(r == 0)
+            def _():
+                for j, rows in enumerate(part_rows):
+                    left_ref[phase, rows] = root_part(rows, slice(0, BS))
+                    left_copy(2 * h + j).start()
+
+            @pl.when(r == 1)
+            def _():
+                for rows in halves:
+                    right_ref[phase, h, rows] = root_part(rows, halves[h])
+                right_copy(h).start()
+
+            yield
+        for h in range(2):
+
+            @pl.when(r == 0)
+            def _():
+                mixed_ref[halves[h]] = dot(left_ref[phase, halves[h]], side[...]).astype(BF16)
+
+            @pl.when(r == 1)
+            def _():
+                for rows in halves:
+                    mixed_ref[rows, halves[h]] = (
+                        dot(gathered[phase, 0, rows], right_ref[phase, h, halves[0]])
+                        + dot(gathered[phase, 1, rows], right_ref[phase, h, halves[1]])
+                    ).astype(BF16)
+
+            yield
+        for h, part_rows in enumerate((chunks[:2], chunks[2:])):
+
+            @pl.when(r == 0)
+            def _():
                 right_copy(h).wait_recv()
+                norm = jnp.zeros((1, 1), F32)
                 for rows in halves:
                     update = dot(mixed_ref[rows], right_in[phase, h])
                     norm = norm + total_of(update * update)
                     if h == 0:
                         update_ref[rows] = update
-            put_norm(norm)
-
-        @pl.when(r == 1)
-        def _():
-            for h, cols in enumerate(halves):
-                for rows in halves:
-                    right_ref[phase, h, rows] = root_part(rows, cols)
-                right_copy(h).start()
-            for h, cols in enumerate(halves):
-                for rows in halves:
-                    mixed_ref[rows, cols] = (
-                        dot(gathered[phase, 0, rows], right_ref[phase, h, halves[0]])
-                        + dot(gathered[phase, 1, rows], right_ref[phase, h, halves[1]])
-                    ).astype(BF16)
-            norm = jnp.zeros((1, 1), F32)
-            for j, rows in enumerate(chunks):
-                left_copy(j).wait_recv()
-                update = dot(left_in[phase, rows], mixed_ref[...])
-                norm = norm + total_of(update * update)
-                update_ref[rows] = update[:, HALF:]
-            put_norm(norm)
-
-        scale = jnp.sqrt(grad_squares) / jnp.sqrt(sums_ref[0:1, 0:1] + 1e-06)
+                norms[h] = jnp.broadcast_to(norm, (8, 128))
+
+            @pl.when(r == 1)
+            def _():
+                norm = jnp.zeros((1, 1), F32)
+                for j, rows in enumerate(part_rows):
+                    left_copy(2 * h + j).wait_recv()
+                    update = dot(left_in[phase, rows], mixed_ref[...])
+                    norm = norm + total_of(update * update)
+                    update_ref[rows] = update[:, HALF:]
+                norms[h] = jnp.broadcast_to(norm, (8, 128))
+
+            yield
+        norm = norms[0, 0:1, 0:1] + norms[1, 0:1, 0:1]
+        scale = jnp.sqrt(grad_squares) / jnp.sqrt(norm + 1e-06)
         place = y if phase == 0 else n_data + lax.div(y, 2)
-        yield
         for distance in (4, 3, 5, 2, 6, 1, 7, 0):
             to = lax.rem(y + distance, n_data)
             rows = pl.ds(pl.multiple_of(to * share, share), share)
@@ -433,6 +449,8 @@
         ring_steps(0, 1, j)
     round_wait(1)
     round_signal(2)
+
+
     def advance(stages, count):
         for _ in range(count):
             next(stages)
@@ -462,17 +480,15 @@
     gather(0)
     ring_steps(1, 2, 0)
     ring_steps(1, 2, 1)
-    advance(main, 1)
     ring_steps(1, 2, 2)
-    advance(main, 1)
     ring_steps(1, 2, 3)
-    advance(main, 1)
+    advance(main, 3)
     finish(1, 2)
     finish(1, 0)
-    advance(main, 1)
+    advance(main, 3)
     finish(1, 3)
     finish(1, 1)
-    advance(main, 1)
+    advance(main, 5)
 
     @pl.when(has_tail)
     def _():
@@ -482,7 +498,7 @@
 
     @pl.when(has_tail)
     def _():
-        advance(precondition(1), 6)
+        advance(precondition(1), 12)
 
     def wait_for(ref, sem):
         pltpu.make_async_copy(ref, ref, sem).wait()
@@ -541,6 +557,7 @@
                 vmem((BS, BS), BF16),
                 vmem((BS, BS), F32),
                 vmem((16, 128), F32),
+                vmem((2, 2, 8, 128), F32),
                 vmem((BS, half), F32),
                 vmem((2, BS, half), BF16),
                 dma,

time: 67.1 us -> 66.8 us (level)
  no operation moved by 1% of the time
where the time goes in v4:
time: 66.8 us; the launch traced here: 66.7 us
  Pallas kernels  65.9 us (99%)
  local copies, waits for them, and re-layouts  0.75 us (1%)
    pallas_call x1, Pallas kernels, on_device(): pl.pallas_call(functools.partial(kernel, n_data, n_owners), out_shape=jax...  65.9 us

profile of v4, /device:TPU:1, one launch (start us, length us, event | category | flops | bytes accessed | tf_op | source)
XLA Modules:
  0.0 66.7 jit_solution(1385912232016989745)
XLA Ops:
  0.0 65.9 %refresh.1 = bf16[12,64,256]{2,1,0:T(8,128)(2,1)S(1)} custom-call(bf16[16,2,12,16,256]{4,3,2,1,0:T(8,128)(2,1)} %bitcast.1), custom_call_target="tpu_custom_call" | custom-call | tf_op jit(solution)/shard_map/refresh/pallas_call | solution.py:536
  65.9 0.7 %copy.3 = bf16[12,64,256]{2,1,0:T(8,128)(2,1)} copy(bf16[12,64,256]{2,1,0:T(8,128)(2,1)S(1)} %refresh.1) | data formatting | bytes 786432

commit v5 on v4

--- a/solution.py
+++ b/solution.py
@@ -406,10 +406,10 @@
         norm = norms[0, 0:1, 0:1] + norms[1, 0:1, 0:1]
         scale = jnp.sqrt(grad_squares) / jnp.sqrt(norm + 1e-06)
         place = y if phase == 0 else n_data + lax.div(y, 2)
+        stage[phase] = (update_ref[...] * scale).astype(BF16)
         for distance in (4, 3, 5, 2, 6, 1, 7, 0):
             to = lax.rem(y + distance, n_data)
             rows = pl.ds(pl.multiple_of(to * share, share), share)
-            stage[phase, rows] = (update_ref[rows] * scale).astype(BF16)
             if distance:
                 pltpu.make_async_remote_copy(
                     src_ref=stage.at[phase, rows],

time: 66.8 us -> 66.8 us (level)
  no operation moved by 1% of the time
where the time goes in v5:
time: 66.8 us; the launch traced here: 66.7 us
  Pallas kernels  65.9 us (99%)
  local copies, waits for them, and re-layouts  0.75 us (1%)
    pallas_call x1, Pallas kernels, on_device(): pl.pallas_call(functools.partial(kernel, n_data, n_owners), out_shape=jax...  65.9 us

profile of v5, /device:TPU:1, one launch (start us, length us, event | category | flops | bytes accessed | tf_op | source)
XLA Modules:
  0.0 66.7 jit_solution(2815643396885644544)
XLA Ops:
  0.0 65.9 %refresh.1 = bf16[12,64,256]{2,1,0:T(8,128)(2,1)S(1)} custom-call(bf16[16,2,12,16,256]{4,3,2,1,0:T(8,128)(2,1)} %bitcast.1), custom_call_target="tpu_custom_call" | custom-call | tf_op jit(solution)/shard_map/refresh/pallas_call | solution.py:536
  65.9 0.7 %copy.3 = bf16[12,64,256]{2,1,0:T(8,128)(2,1)} copy(bf16[12,64,256]{2,1,0:T(8,128)(2,1)S(1)} %refresh.1) | data formatting | bytes 786432
